TPU v7x, 512 devices: a whole 4x4x16 slice. The times are simulated.
512 devices in a mesh: net: 64 (over z, x_lo, core), hyd: 8 (over x_hi, y).
Axes of the slice: x: 4 (x_hi: 2, x_lo: 2; x = x_hi * 2 + x_lo), y: 4, z: 16, core: 2. Of those that a mesh axis runs over, the one named last changes fastest.
Arguments:
- diagonal: float32 [32768], P('net'), may hold values from 0.1 to 1
- edge_ends: int32 [40960, 2], P('net'), may hold values from 0 to 511, as said below
- edge_cond: float32 [40960], P('net'), may hold values from 0.3 to 3
- bnd_nodes: int32 [64, 2, 64], P('net'), may hold values from 0 to 511
- bnd_cond: float32 [64, 2, 64], P('net'), may hold values from 0 to 3, as said below
- hyd_ids: int32 [2048], P('hyd'), may hold values from 0 to 32767
- warm_start: float32 [32768, 2048], P('net', 'hyd'), may hold values from -6 to 6
- scen_picks: int32 [1024, 4], replicated, may hold values from 0 to 2047
- scen_flows: float32 [1024, 4], replicated, may hold values from 0.5 to 2
Outputs:
- responses: float32 [32768, 2048], P('net', 'hyd')
- heads: float32 [1024, 32768], P('hyd', 'net')
Inputs may be any that keep to these rules, and one draw needn't show every extreme that they name: `edge_ends`: in each partition's block of 640 rows the first 511 rows join all the partition's nodes in one path; no row joins a node to itself. `bnd_cond`: entry [p, 1, k] equals entry [p + 1, 0, k]; row 0 of the first partition and row 1 of the last are zero, all other entries positive.
All inputs are finite; a program needn't handle non-finite values.
Results may differ from a plain program's by a relative error of at most 0.0003.
Values sent between devices are 32-bit elements; how exact they have to be, the bound alone decides.
A program may use at most 64 MiB of HBM per device.

v0:
```python
import jax
import jax.numpy as jnp
from jax import lax
from jax.sharding import PartitionSpec as P

PICK = 4
ITERS = 2


def padded(shard, sides, width):
    for axis, dim in sides:
        devices, length = (lax.axis_size(axis), shard.shape[dim])
        up = [(i, (i + 1) % devices) for i in range(devices - 1)]
        down = [(j, i) for i, j in up]
        last = lax.slice_in_dim(shard, length - width, length, axis=dim)
        leading = lax.slice_in_dim(shard, 0, width, axis=dim)
        before = lax.ppermute(last, axis, up)
        after = lax.ppermute(leading, axis, down)
        shard = jnp.concatenate([before, shard, after], axis=dim)
    return shard


def local_matrix(diagonal, edge_ends, edge_cond):
    node_count = diagonal.shape[0]
    node_iota = jnp.arange(node_count, dtype=jnp.int32)
    incidence = (edge_ends[:, 0:1] == node_iota[None, :]).astype(jnp.float32) - (
        edge_ends[:, 1:2] == node_iota[None, :]
    ).astype(jnp.float32)
    weighted = edge_cond[:, None] * incidence
    laplace = lax.dot_general(
        incidence, weighted, (((0,), (0,)), ((), ())), precision=lax.Precision.HIGHEST
    )
    return laplace + jnp.diag(diagonal)


def apply_matrix(values, dense_op, bnd_nodes, bnd_cond):
    rim_size = bnd_nodes.shape[2]
    lower_ids = bnd_nodes[0, 0]
    upper_ids = bnd_nodes[0, 1]
    lower_rows = values[lower_ids]
    upper_rows = values[upper_ids]
    widened = padded(jnp.concatenate([lower_rows, upper_rows], 0), (("net", 0),), rim_size)
    before_rows = widened[:rim_size]
    after_rows = widened[3 * rim_size :]
    result = jnp.dot(dense_op, values, precision=lax.Precision.HIGHEST)
    result = result.at[lower_ids].add(bnd_cond[0, 0][:, None] * (lower_rows - before_rows))
    result = result.at[upper_ids].add(bnd_cond[0, 1][:, None] * (upper_rows - after_rows))
    return result


def gram_of(first_m, second_m):
    return lax.dot_general(
        first_m, second_m, (((0,), (0,)), ((), ())), precision=lax.Precision.HIGHEST
    )


def times_of(first_m, second_m):
    return jnp.dot(first_m, second_m, precision=lax.Precision.HIGHEST)


def solve_spd(matrix, rhs_m):
    factor = jnp.linalg.cholesky(matrix)
    return jax.scipy.linalg.cho_solve((factor, True), rhs_m)


def residual_sum(residual):
    return lax.psum(gram_of(residual, residual), "net")


def per_device(
    diagonal, edge_ends, edge_cond, bnd_nodes, bnd_cond, hyd_ids, warm_start, scen_picks, scen_flows
):
    node_count = warm_start.shape[0]
    block_cols = warm_start.shape[1]
    dense_op = local_matrix(diagonal, edge_ends, edge_cond)

    def operator(values):
        return apply_matrix(values, dense_op, bnd_nodes, bnd_cond)

    node_base = lax.axis_index("net") * node_count
    local_ids = hyd_ids - node_base
    node_iota = jnp.arange(node_count, dtype=jnp.int32)
    demand = (node_iota[:, None] == local_ids[None, :]).astype(jnp.float32)
    iterate = warm_start
    residual = demand - operator(iterate)
    direction = residual
    res_gram = residual_sum(residual)
    for sweep in range(ITERS):
        image = operator(direction)
        dir_gram = lax.psum(gram_of(direction, image), "net")
        alpha_m = solve_spd(dir_gram, res_gram)
        iterate = iterate + times_of(direction, alpha_m)
        residual = residual - times_of(image, alpha_m)
        if sweep + 1 < ITERS:
            new_gram = residual_sum(residual)
            beta_m = solve_spd(res_gram, new_gram)
            direction = residual + times_of(direction, beta_m)
            res_gram = new_gram
    groups = lax.axis_size("hyd")
    total_hyd = block_cols * groups
    scen_total = scen_picks.shape[0]
    scen_local = scen_total // groups
    scen_start = lax.axis_index("hyd") * scen_local
    picks_mine = lax.dynamic_slice_in_dim(scen_picks, scen_start, scen_local, 0)
    flows_mine = lax.dynamic_slice_in_dim(scen_flows, scen_start, scen_local, 0)
    hyd_iota = jnp.arange(total_hyd, dtype=jnp.int32)
    scenario = jnp.zeros((total_hyd, scen_local), jnp.float32)
    for slot in range(PICK):
        scenario = scenario + flows_mine[:, slot][None, :] * (
            hyd_iota[:, None] == picks_mine[:, slot][None, :]
        ).astype(jnp.float32)
    initial = jnp.zeros((scen_local, node_count), jnp.float32)
    heads = initial + lax.dot_general(
        scenario,
        lax.all_gather(iterate, "hyd", axis=1, tiled=True),
        (((0,), (1,)), ((), ())),
        precision=lax.Precision.HIGHEST,
    )
    return (iterate, heads)


def solution(mesh):
    placed = (
        P("net"),
        P("net", None),
        P("net"),
        P("net", None, None),
        P("net", None, None),
        P("hyd"),
        P("net", "hyd"),
        P(),
        P(),
    )
    return jax.shard_map(
        per_device,
        mesh=mesh,
        in_specs=placed,
        out_specs=(P("net", "hyd"), P("hyd", "net")),
        check_vma=False,
    )
```

profile of v0, /device:TPU:1, one launch (start us, length us, event | category | flops | bytes accessed | tf_op | source)
XLA Modules:
  0.0 1586.7 jit_solution(7142381146179333786)
XLA Ops:
  9.7 4.5 collective-permute-start
  15.9 5.6 collective-permute-start.1
  23.1 4.2 fusion.2
  33.2 1.9 collective-permute-start.3
  35.1 3.6 collective-permute-start.2
  38.8 1.7 fusion.104
  45.5 440.8 %all-reduce.10.cloned.1.call-done = (f32[256,256]{0,1:T(8,128)}, f32[256,256]{0,1:T(8,128)}) async-done(((f32[256,256]{0,1:T(8,128)}, f32[256,256]{0,1:T(8,128)}), (f32[256,256]{0,1:T(8,128)}, f32[256,256]{0,1:T(8,128)})) %all-reduce.10.cloned.1.call-update) | async-done | bytes 524304 | tf_op jit(solution)/shard_map/psum | solution.py:67
  488.5 1.8 fusion.35
  491.2 11.7 cholesky.206
  502.9 11.7 cholesky.172
  515.3 10.4 custom-call.17
  526.5 10.2 custom-call.19
  538.9 11.7 cholesky.223
  553.5 11.7 cholesky.189
  567.9 4.2 while.6
  572.1 19.7 %custom-call.18 = f32[2,128,128]{1,2,0:T(8,128)S(1)} custom-call(f32[2,128,128]{2,1,0:T(8,128)S(1)} %get-tuple-element.24), custom_call_target="InvertDiagBlocksLowerTriangular" | custom-call | tf_op jit(solution)/shard_map/jit(_cho_solve)/triangular_solve | solution.py:63
  594.3 1.7 fusion.105
  597.4 4.0 while.7
  601.3 19.7 %custom-call.20 = f32[2,128,128]{1,2,0:T(8,128)S(1)} custom-call(f32[2,128,128]{2,1,0:T(8,128)S(1)} %get-tuple-element.25), custom_call_target="InvertDiagBlocksLowerTriangular" | custom-call | tf_op jit(solution)/shard_map/jit(_cho_solve)/triangular_solve | solution.py:63
  621.0 378.3 %all-reduce.6.cloned.1.call-done = f32[256,256]{1,0:T(8,128)} async-done(((f32[256,256]{1,0:T(8,128)}), f32[256,256]{1,0:T(8,128)}) %all-reduce.6.cloned.1.call-update) | async-done | bytes 262160 | tf_op jit(solution)/shard_map/psum | solution.py:67
  1005.1 2.3 collective-permute-start.5
  1007.4 3.3 collective-permute-start.4
  1013.5 1.7 scatter_custom_fusion.5
  1015.2 1.7 fusion.107
  1017.6 404.7 %all-reduce.8.cloned.1.call-done = f32[256,256]{0,1:T(8,128)} async-done(((f32[256,256]{0,1:T(8,128)}), f32[256,256]{0,1:T(8,128)}) %all-reduce.8.cloned.1.call-update) | async-done | bytes 262160 | tf_op jit(solution)/shard_map/psum | solution.py:90
  1424.5 11.7 cholesky.240
  1436.8 9.8 custom-call.21
  1447.2 11.7 cholesky.257
  1461.0 4.3 while.8
  1465.2 19.7 %custom-call.22 = f32[2,128,128]{1,2,0:T(8,128)S(1)} custom-call(f32[2,128,128]{2,1,0:T(8,128)S(1)} %get-tuple-element.26), custom_call_target="InvertDiagBlocksLowerTriangular" | custom-call | tf_op jit(solution)/shard_map/jit(_cho_solve)/triangular_solve | solution.py:63
  1488.8 83.2 %all-gather.2.cloned.1.call-done = f32[512,2048]{1,0:T(8,128)} async-done(((f32[512,256]{1,0:T(8,128)}), f32[512,2048]{1,0:T(8,128)}) %all-gather.2.cloned.1.call-update) | async-done | bytes 4194320 | tf_op jit(solution)/shard_map/all_gather | solution.py:115
  1572.0 7.7 fusion.8
  (148 shorter events, 58.7 us)
Async XLA Ops:
  7.2 1480.9 %copy-start = (s32[1024,4]{0,1:T(4,128)S(1)}, s32[1024,4]{0,1:T(4,128)}, u32[]{:S(2)}) copy-start(s32[1024,4]{0,1:T(4,128)} %param.19) | copy-start | bytes 49156
  7.2 479.1 %all-reduce.10.cloned.1.call-start = ((), (), s32[]{:S(2)}) async-start(), calls=%async_computation.3 | async-start | bytes 1048576 | tf_op jit(solution)/shard_map/psum | solution.py:67
  8.0 32.5 %copy-start.12 = (s32[64]{0:T(128)}, s32[64]{0:T(128)S(1)}, u32[]{:S(2)}) copy-start(s32[64]{0:T(128)S(1)} %get-tuple-element.84) | copy-start | bytes 772
  8.0 33.8 %copy-start.11 = (s32[64]{0:T(128)}, s32[64]{0:T(128)S(1)}, u32[]{:S(2)}) copy-start(s32[64]{0:T(128)S(1)} %get-tuple-element.83) | copy-start | bytes 772
  8.0 22.9 %copy-start.9 = (s32[1024]{0:T(1024)}, s32[1024]{0:T(1024)S(1)}, u32[]{:S(2)}) copy-start(s32[1024]{0:T(1024)S(1)} %pad_clamp_fusion) | copy-start | bytes 12292
  9.7 18.6 %collective-permute-start = (f32[64,256]{1,0:T(8,128)S(1)}, f32[64,256]{1,0:T(8,128)S(1)}, u32[]{:S(2)}, u32[]{:S(2)}) collective-permute-start(f32[64,256]{1,0:T(8,128)S(1)} %gather_fusion.1), channel_id=1, source_target_pairs={{0,8},{8,16},{16,24},{24,32},{32,40},{40,48},{48,56},{56,64},{64,7... | collective-permute-start | bytes 196616 | tf_op jit(solution)/shard_map/ppermute | solution.py:17
  14.2 17.3 %copy-start.10 = (s32[1024]{0:T(1024)}, s32[1024]{0:T(1024)S(1)}, u32[]{:S(2)}) copy-start(s32[1024]{0:T(1024)S(1)} %pad_clamp_fusion.1) | copy-start | bytes 12292
  15.9 13.6 collective-permute-start.1
  22.3 18.2 %copy-start.8 = (f32[64]{0:T(128)}, f32[64]{0:T(128)S(1)}, u32[]{:S(2)}) copy-start(f32[64]{0:T(128)S(1)} %get-tuple-element.82) | copy-start | bytes 772
  22.3 19.5 %copy-start.7 = (f32[64]{0:T(128)}, f32[64]{0:T(128)S(1)}, u32[]{:S(2)}) copy-start(f32[64]{0:T(128)S(1)} %get-tuple-element.81) | copy-start | bytes 772
  23.1 4.2 copy-start.1
  27.3 1.0 copy-start.13
  33.2 8.5 collective-permute-start.3
  35.1 5.4 collective-permute-start.2
  44.7 954.6 %all-reduce.6.cloned.1.call-start = ((), (), s32[]{:S(2)}) async-start(), calls=%async_computation | async-start | bytes 524288 | tf_op jit(solution)/shard_map/psum | solution.py:67
  490.3 60.4 %copy-start.6 = (f32[256,256]{1,0:T(8,128)}, f32[256,256]{1,0:T(8,128)S(1)}, u32[]{:S(2)}) copy-start(f32[256,256]{1,0:T(8,128)S(1)} %get-tuple-element.92) | copy-start | bytes 786436
  550.6 41.2 %copy-start.2 = (f32[256,256]{0,1:T(8,128)S(1)}, f32[256,256]{0,1:T(8,128)}, u32[]{:S(2)}) copy-start(f32[256,256]{0,1:T(8,128)} %get-tuple-element.53) | copy-start | bytes 786436
  550.6 16.6 %copy-start.4 = (f32[256,256]{1,0:T(8,128)}, f32[256,256]{1,0:T(8,128)S(1)}, u32[]{:S(2)}) copy-start(f32[256,256]{1,0:T(8,128)S(1)} %get-tuple-element.66) | copy-start | bytes 786436
  594.3 3.1 copy-start.5
  596.0 826.3 %all-reduce.8.cloned.1.call-start = ((), (), s32[]{:S(2)}) async-start(), calls=%async_computation.1 | async-start | bytes 524288 | tf_op jit(solution)/shard_map/psum | solution.py:90
  601.3 401.6 %copy-start.14 = (s32[2,2]{1,0:T(2,128)}, s32[2,2]{1,0:T(2,128)S(1)}, u32[]{:S(2)}) copy-start(s32[2,2]{1,0:T(2,128)S(1)} %get-tuple-element.261) | copy-start | bytes 52
  1005.1 8.4 collective-permute-start.5
  1007.4 4.6 collective-permute-start.4
  1017.0 555.1 %all-gather.2.cloned.1.call-start = ((), (), s32[]{:S(2)}) async-start(), calls=%async_computation.2 | async-start | bytes 4718592 | tf_op jit(solution)/shard_map/all_gather | solution.py:115
  1423.4 37.5 %copy-start.15 = (s32[2,2]{1,0:T(2,128)S(1)}, s32[2,2]{1,0:T(2,128)}, u32[]{:S(2)}) copy-start(s32[2,2]{1,0:T(2,128)} %copy-done.14) | copy-start | bytes 52
  1436.2 48.7 %copy-start.3 = (f32[256,256]{1,0:T(8,128)S(1)}, f32[256,256]{1,0:T(8,128)}, u32[]{:S(2)}) copy-start(f32[256,256]{1,0:T(8,128)} %all-reduce.6.cloned.1.call-done) | copy-start | bytes 786436
Sparse Core Ops, SparseCore 0:
  44.8 441.4 all-reduce.9
  596.1 403.1 all-reduce.5
  1017.1 405.2 all-reduce.7
  1488.2 83.8 all-gather.1
where the time goes:
time: 1600 us; the launch traced here: 1590 us
  waiting for transfers between devices  1310 us (82%)
  other arithmetic  176 us (11%)
  matrix products  36.6 us (2%)
  local copies, waits for them, and re-layouts  25.2 us (2%)
  starting transfers between devices  21.6 us (1%)
  between operations  18.8 us (1%)
    psum x2, waiting for transfers between devices, residual_sum(): return lax.psum(gram_of(residual, residual), 'net')  819 us
    psum x1, waiting for transfers between devices, per_device(): dir_gram = lax.psum(gram_of(direction, image), 'net')  405 us
    another operation x21, other arithmetic, solve_spd(): factor = jnp.linalg.cholesky(matrix)  105 us
    all_gather x1, waiting for transfers between devices, per_device(): lax.all_gather(iterate, 'hyd', axis=1, tiled=True)  83.2 us
    another operation x7, other arithmetic, solve_spd(): return jax.scipy.linalg.cho_solve((factor, True), rhs_m)  59.6 us
  transfers between devices with their start and end apart: 10, of which 5 were waited for; matrix products, arithmetic and copies ran while one was open for 3% of the time, Pallas kernels for 0%

commit v1 on v0

v1 whole, which is shorter than its diff:
```python
import functools

import jax
import jax.numpy as jnp
from jax import lax
from jax.experimental import pallas as pl
from jax.experimental.pallas import tpu as pltpu
from jax.sharding import PartitionSpec as P

MESH = pl.DeviceIdType.MESH
F32 = jnp.float32
BF16 = jnp.bfloat16
NN = (((1,), (0,)), ((), ()))
TN = (((0,), (0,)), ((), ()))
NT = (((1,), (1,)), ((), ()))
PICK = 4


def pieces(value, count):
    out = []
    for step in range(count):
        part = value.astype(BF16)
        out.append(part)
        if step + 1 < count:
            value = value - part.astype(F32)
    return out


def dot_pieces(first, second, dims):
    depth = max(len(first), len(second))
    total = None
    for level in reversed(range(depth)):
        for i, left in enumerate(first):
            j = level - i
            if 0 <= j < len(second):
                term = lax.dot_general(left, second[j], dims, preferred_element_type=F32)
                total = term if total is None else total + term
    return total


def dot_full(first, second, dims=NN):
    return lax.dot_general(
        first, second, dims, precision=lax.Precision.HIGHEST, preferred_element_type=F32
    )


def dot_one(first, second):
    return lax.dot_general(
        first.astype(BF16), second.astype(BF16), NN, preferred_element_type=F32
    )


def moments_kernel(
    nz,
    diag_ref,
    ends_ref,
    cond_ref,
    bn_ref,
    bc_ref,
    hid_ref,
    x_ref,
    r_ref,
    q_ref,
    t_out,
    d_out,
    a_ref,
    halo_src,
    halo_dst,
    t_buf,
    d_buf,
    core_t,
    core_d,
    acc_t,
    acc_d,
    zr_t,
    zr_d,
    xs,
    xr,
    halo_ss,
    halo_rs,
    core_ss,
    core_rs,
    zr_ss,
    zr_rs,
    x_ss,
    x_rs,
    ag_ss,
    ag_rs,
    fin_ss,
    fin_rs,
):
    nodes, cols = x_ref.shape
    edges = cond_ref.shape[1]
    rim = bn_ref.shape[1]
    n_net = 4 * nz
    net = lax.axis_index("net")
    z = net // 4
    x_lo = lax.rem(net // 2, 2)
    core = lax.rem(net, 2)
    up, down = lax.rem(net + 1, n_net), lax.rem(net + n_net - 1, n_net)
    core_mate = net + 1 - 2 * core
    x_mate = net + 2 - 4 * x_lo

    def z_mate(step):
        return lax.rem(net + 4 * step, n_net)

    barrier = pltpu.get_barrier_semaphore()
    order = sorted(range(1, nz), key=lambda s: -min(s, nz - s))
    mates = [z_mate(s) for s in order] + [x_mate, up, down]
    for mate in mates:
        pl.semaphore_signal(barrier, inc=1, device_id={"net": mate}, device_id_type=MESH)

    def remote(src, dst, ss, rs, mate):
        return pltpu.make_async_remote_copy(
            src_ref=src,
            dst_ref=dst,
            send_sem=ss,
            recv_sem=rs,
            device_id={"net": mate},
            device_id_type=MESH,
        )

    node_iota = lax.broadcasted_iota(jnp.int32, (nodes, edges), 0)
    first = node_iota == ends_ref[0:1, :]
    second = node_iota == ends_ref[1:2, :]
    incidence = first.astype(F32) - second.astype(F32)
    ids = jnp.concatenate([bn_ref[0:1, :], bn_ref[1:2, :]], axis=1)
    conds = jnp.concatenate([bc_ref[0:1, :], bc_ref[1:2, :]], axis=1)
    pick = (lax.broadcasted_iota(jnp.int32, (nodes, 2 * rim), 0) == ids).astype(F32)
    pick_b = [pick.astype(BF16)]
    x_parts = pieces(x_ref[...], 3)

    def gather(parts, stage):
        halo_src[stage] = dot_pieces(pick_b, parts, TN)

    gather(x_parts, 0)
    incidence_b = incidence.astype(BF16)
    total = None
    for part in reversed(pieces(cond_ref[...], 3)):
        term = lax.dot_general(
            (incidence * part.astype(F32)).astype(BF16), incidence_b, NT, preferred_element_type=F32
        )
        total = term if total is None else total + term
    for part in reversed(pieces(conds, 3)):
        total = total + lax.dot_general(
            (pick * part.astype(F32)).astype(BF16), pick_b[0], NT, preferred_element_type=F32
        )
    square = lax.broadcasted_iota(jnp.int32, (nodes, nodes), 0) == lax.broadcasted_iota(
        jnp.int32, (nodes, nodes), 1
    )
    a_ref[...] = total + jnp.where(square, diag_ref[...], 0.0)
    couple = pieces(pick * conds, 3)

    pl.semaphore_wait(barrier, len(mates))

    def halo(stage):
        upper, lower = pl.ds(rim, rim), pl.ds(0, rim)
        return [
            remote(
                halo_src.at[stage, upper],
                halo_dst.at[stage, lower],
                halo_ss.at[2 * stage],
                halo_rs.at[2 * stage],
                up,
            ),
            remote(
                halo_src.at[stage, lower],
                halo_dst.at[stage, upper],
                halo_ss.at[2 * stage + 1],
                halo_rs.at[2 * stage + 1],
                down,
            ),
        ]

    def local(parts):
        return dot_pieces(pieces(a_ref[...], 3), parts, NN)

    def coupled(stage):
        return dot_pieces(couple, pieces(halo_dst[stage], 3), NN)

    halos = [halo(stage) for stage in range(3)]
    for copy in halos[0]:
        copy.start()
    hyd_local = hid_ref[...] - net * nodes
    demand = (lax.broadcasted_iota(jnp.int32, (nodes, cols), 0) == hyd_local).astype(F32)
    part_r = demand - local(x_parts)
    for copy in halos[0]:
        copy.wait_recv()
    residual = part_r + coupled(0)
    r_parts = pieces(residual, 3)
    gather(r_parts, 1)
    for copy in halos[1]:
        copy.start()
    r_ref[...] = residual
    part_q = local(r_parts)
    m0 = dot_pieces(r_parts, r_parts, TN)
    for copy in halos[1]:
        copy.wait_recv()
    image = part_q - coupled(1)
    q_parts = pieces(image, 3)
    gather(q_parts, 2)
    for copy in halos[2]:
        copy.start()
    q_ref[...] = image

    row = lax.broadcasted_iota(jnp.int32, (cols, cols), 0)
    col = lax.broadcasted_iota(jnp.int32, (cols, cols), 1)

    half = cols // 2
    chunk = half // nz

    def pack(lot, upper_m, lower_m):
        t_buf[lot] = jnp.where(row <= col, upper_m, lower_m)
        diagonal = jnp.sum(jnp.where(row == col, lower_m, 0.0), axis=0, keepdims=True)
        d_buf[lot] = jnp.broadcast_to(diagonal, (8, cols))

    def core_copies(lot):
        other = pl.ds(pl.multiple_of((1 - core) * half, half), half)
        return [
            remote(
                t_buf.at[lot, other],
                core_t.at[lot],
                core_ss.at[2 * lot],
                core_rs.at[2 * lot],
                core_mate,
            ),
            remote(
                d_buf.at[lot],
                core_d.at[lot],
                core_ss.at[2 * lot + 1],
                core_rs.at[2 * lot + 1],
                core_mate,
            ),
        ]

    def core_sum(lot):
        mine = pl.ds(pl.multiple_of(core * half, half), half)
        acc_t[lot] = t_buf[lot, mine] + core_t[lot]
        acc_d[lot] = d_buf[lot] + core_d[lot]

    owner_z = [nz // 4, (3 * nz) // 4]

    def z_copies(lot):
        out = []
        for step in order:
            owner = lax.rem(z + step, nz)
            rows = pl.ds(pl.multiple_of(owner * chunk, chunk), chunk)
            out.append(
                remote(
                    acc_t.at[lot, rows],
                    zr_t.at[lot, step - 1],
                    zr_ss.at[lot, step - 1],
                    zr_rs.at[lot, step - 1],
                    z_mate(step),
                )
            )
        return out

    def d_copy(lot, slot, mate):
        return remote(
            acc_d.at[lot],
            zr_d.at[lot, slot],
            zr_ss.at[lot, nz - 1],
            zr_rs.at[lot, nz - 1 + slot],
            mate,
        )

    def z_start(lot):
        for copy in z_copies(lot):
            copy.start()
        to_owner = lax.rem(owner_z[lot] - z + nz, nz)

        @pl.when(to_owner != 0)
        def _():
            d_copy(lot, to_owner - 1, lax.rem(net + 4 * to_owner, n_net)).start()

    def x_copy(lot):
        return remote(xs.at[lot], xr.at[lot], x_ss.at[lot], x_rs.at[lot], x_mate)

    def z_sum(lot):
        for copy in z_copies(lot):
            copy.wait_recv()
        mine = pl.ds(pl.multiple_of(z * chunk, chunk), chunk)
        total = acc_t[lot, mine]
        for step in range(1, nz):
            total = total + zr_t[lot, step - 1]
        xs[lot, 0:chunk] = total
        xs[lot, chunk : chunk + 8] = acc_d[lot]

        @pl.when(z == owner_z[lot])
        def _():
            total_d = acc_d[lot]
            for slot in range(nz - 1):
                d_copy(lot, slot, z_mate(slot + 1)).wait_recv()
            for slot in range(nz - 1):
                total_d = total_d + zr_d[lot, slot]
            xs[lot, chunk : chunk + 8] = total_d

        x_copy(lot).start()

    def full_rows(index):
        return pl.ds(pl.multiple_of(core * half + index * chunk, chunk), chunk)

    def ag_copies(lot, received):
        out = []
        for step in order:
            owner = lax.rem(z + nz - step, nz) if received else z
            out.append(
                remote(
                    t_out.at[lot, full_rows(owner)],
                    t_out.at[lot, full_rows(owner)],
                    ag_ss.at[lot, step - 1],
                    ag_rs.at[lot, step - 1],
                    z_mate(step),
                )
            )
        return out

    def agd_copy(lot, step):
        return remote(
            d_out.at[lot],
            d_out.at[lot],
            ag_ss.at[lot, nz - 1 + step - 1],
            ag_rs.at[lot, nz - 1],
            z_mate(step),
        )

    def x_sum(lot):
        x_copy(lot).wait_recv()
        t_out[lot, full_rows(z)] = xs[lot, 0:chunk] + xr[lot, 0:chunk]

        @pl.when(z == owner_z[lot])
        def _():
            d_out[lot] = xs[lot, chunk : chunk + 8] + xr[lot, chunk : chunk + 8]
            for step in order:
                agd_copy(lot, step).start()

        for copy in ag_copies(lot, False):
            copy.start()

    def fin_copy(lot, whose):
        rows = pl.ds(pl.multiple_of(whose * half, half), half)
        return remote(
            t_out.at[lot, rows], t_out.at[lot, rows], fin_ss.at[lot], fin_rs.at[lot], core_mate
        )

    def ag_finish(lot):
        for copy in ag_copies(lot, True):
            copy.wait_recv()
        fin_copy(lot, core).start()

        @pl.when(z != owner_z[lot])
        def _():
            agd_copy(lot, 1).wait_recv()

    def finish(lot):
        fin_copy(lot, 1 - core).wait_recv()

    def drain(lot):
        for copy in core_copies(lot):
            copy.wait_send()
        for copy in z_copies(lot):
            copy.wait_send()
        x_copy(lot).wait_send()
        for copy in ag_copies(lot, False):
            copy.wait_send()
        fin_copy(lot, core).wait_send()

        @pl.when(z != owner_z[lot])
        def _():
            d_copy(lot, 0, z_mate(1)).wait_send()

        @pl.when(z == owner_z[lot])
        def _():
            for step in order:
                agd_copy(lot, step).wait_send()

    pack(0, m0, dot_pieces(r_parts, q_parts, TN))
    for copy in core_copies(0):
        copy.start()
    part_w = local(q_parts)
    for copy in core_copies(0):
        copy.wait_recv()
    core_sum(0)
    z_start(0)
    m2 = dot_pieces(q_parts, q_parts, TN)
    for copy in halos[2]:
        copy.wait_recv()
    m3 = dot_pieces(q_parts, pieces(part_w - coupled(2), 3), TN)
    pack(1, m2, m3)
    for copy in core_copies(1):
        copy.start()
    for copy in core_copies(1):
        copy.wait_recv()
    core_sum(1)
    z_start(1)
    z_sum(0)
    x_sum(0)
    z_sum(1)
    x_sum(1)
    ag_finish(0)
    ag_finish(1)
    finish(0)
    finish(1)
    for stage in halos:
        for copy in stage:
            copy.wait_send()
    drain(0)
    drain(1)


def moments(diagonal, edge_ends, edge_cond, bnd_nodes, bnd_cond, hyd_ids, warm_start, n_net):
    nz = n_net // 4
    nodes, cols = warm_start.shape
    rim = bnd_nodes.shape[2]
    chunk = cols // 2 // nz
    dma = pltpu.SemaphoreType.DMA
    vmem = pl.BlockSpec(memory_space=pltpu.VMEM)
    return pl.pallas_call(
        functools.partial(moments_kernel, nz),
        name="moments",
        out_shape=[
            jax.ShapeDtypeStruct((nodes, cols), F32),
            jax.ShapeDtypeStruct((nodes, cols), F32),
            jax.ShapeDtypeStruct((2, cols, cols), F32),
            jax.ShapeDtypeStruct((2, 8, cols), F32),
        ],
        in_specs=[vmem] * 7,
        out_specs=[vmem] * 4,
        scratch_shapes=[
            pltpu.VMEM((nodes, nodes), F32),
            pltpu.VMEM((3, 2 * rim, cols), F32),
            pltpu.VMEM((3, 2 * rim, cols), F32),
            pltpu.VMEM((2, cols, cols), F32),
            pltpu.VMEM((2, 8, cols), F32),
            pltpu.VMEM((2, cols // 2, cols), F32),
            pltpu.VMEM((2, 8, cols), F32),
            pltpu.VMEM((2, cols // 2, cols), F32),
            pltpu.VMEM((2, 8, cols), F32),
            pltpu.VMEM((2, nz - 1, chunk, cols), F32),
            pltpu.VMEM((2, nz - 1, 8, cols), F32),
            pltpu.VMEM((2, chunk + 8, cols), F32),
            pltpu.VMEM((2, chunk + 8, cols), F32),
            dma((6,)),
            dma((6,)),
            dma((4,)),
            dma((4,)),
            dma((2, nz)),
            dma((2, 2 * nz - 2)),
            dma((2,)),
            dma((2,)),
            dma((2, 2 * nz - 2)),
            dma((2, nz)),
            dma((2,)),
            dma((2,)),
        ],
        compiler_params=pltpu.CompilerParams(
            collective_id=0, has_side_effects=True, vmem_limit_bytes=48 << 20
        ),
    )(
        diagonal[None, :],
        edge_ends.T,
        edge_cond[None, :],
        bnd_nodes[0],
        bnd_cond[0],
        hyd_ids[None, :],
        warm_start,
    )


def update_kernel(x_ref, r_ref, q_ref, t_ref, d_ref, out_ref, inv_ref):
    size = t_ref.shape[1]
    row = lax.broadcasted_iota(jnp.int32, (size, size), 0)
    col = lax.broadcasted_iota(jnp.int32, (size, size), 1)
    eye = (row == col).astype(F32)

    def unpack(lot):
        packed = t_ref[lot]
        upper = jnp.where(row < col, packed, 0.0)
        lower = jnp.where(row > col, packed, 0.0)
        first = jnp.where(row <= col, packed, 0.0) + upper.T
        second = lower + lower.T + eye * d_ref[lot, 0:1, :]
        return first, second

    def inverse(matrix):
        diag = eye * matrix
        by_row = lax.rsqrt(jnp.sum(diag, axis=1, keepdims=True))
        by_col = lax.rsqrt(jnp.sum(diag, axis=0, keepdims=True))
        scaled = matrix * by_row * by_col
        bound = jnp.max(jnp.sum(jnp.abs(scaled), axis=0, keepdims=True), axis=1, keepdims=True)
        gain = 2.0 / bound
        start = eye * gain
        error = eye - scaled * gain
        approx = start + error * gain
        for _ in range(5):
            error = dot_one(error, error)
            approx = approx + dot_one(approx, error)
        rest = eye - dot_full(scaled, approx)
        size_of = jnp.sum(rest * rest)
        good = size_of < 0.25
        inv_ref[...] = jnp.where(good, approx + dot_full(approx, rest), start)

        def unfinished(state):
            step, size_of = state
            return jnp.logical_and(step < 64, jnp.logical_not(size_of < 1e-6))

        def improve(state):
            approx = inv_ref[...]
            rest = eye - dot_full(scaled, approx)
            inv_ref[...] = approx + dot_full(approx, rest)
            return state[0] + 1, jnp.sum(rest * rest)

        lax.while_loop(unfinished, improve, (jnp.int32(0), size_of))
        return inv_ref[...] * by_row * by_col

    m0, m1 = unpack(0)
    m2, m3 = unpack(1)
    inv1 = inverse(m1)
    alpha = dot_full(inv1, m0)
    cross = dot_full(inv1, m2)
    schur = m3 - dot_full(m2, cross)
    rhs = m1 - dot_full(m2, alpha)
    weight_q = dot_full(inverse(schur), rhs)
    weight_r = alpha - dot_full(cross, weight_q)
    out_ref[...] = (
        x_ref[...]
        + dot_pieces(pieces(r_ref[...], 3), pieces(weight_r, 3), NN)
        + dot_pieces(pieces(q_ref[...], 3), pieces(weight_q, 3), NN)
    )


def update(warm_start, residual, image, packed, diagonals):
    cols = warm_start.shape[1]
    vmem = pl.BlockSpec(memory_space=pltpu.VMEM)
    return pl.pallas_call(
        update_kernel,
        name="update",
        out_shape=jax.ShapeDtypeStruct(warm_start.shape, F32),
        in_specs=[vmem] * 5,
        out_specs=vmem,
        scratch_shapes=[pltpu.VMEM((cols, cols), F32)],
        compiler_params=pltpu.CompilerParams(vmem_limit_bytes=48 << 20),
    )(warm_start, residual, image, packed, diagonals)


def heads_kernel(groups, x_ref, picks_ref, flows_ref, out_ref, src, dst, ss, rs):
    nodes, cols = x_ref.shape
    scen = out_ref.shape[0]
    hyd = lax.axis_index("hyd")
    order = sorted(range(1, groups), key=lambda s: -min(s % 4, 4 - s % 4) - 2 * (s >= 4))
    order = order[: groups - 1]

    def mate(step):
        return lax.rem(hyd + step, groups)

    barrier = pltpu.get_barrier_semaphore()
    for step in order:
        pl.semaphore_signal(barrier, inc=1, device_id={"hyd": mate(step)}, device_id_type=MESH)

    x_parts = pieces(x_ref[...], 3)
    column = lax.broadcasted_iota(jnp.int32, (cols, scen), 0) + hyd * cols

    def scenario(owner):
        lanes = pl.ds(pl.multiple_of(owner * scen, scen), scen)
        picks, flows = picks_ref[:, lanes], flows_ref[:, lanes]
        total = jnp.zeros((cols, scen), F32)
        for slot in range(PICK):
            total = total + jnp.where(
                column == picks[slot : slot + 1, :], flows[slot : slot + 1, :], 0.0
            )
        return total

    def copy(step):
        return pltpu.make_async_remote_copy(
            src_ref=src.at[step],
            dst_ref=dst.at[step],
            send_sem=ss.at[step],
            recv_sem=rs.at[step],
            device_id={"hyd": mate(step)},
            device_id_type=MESH,
        )

    every = order + [0]
    waited = False
    for at in range(0, len(every), 2):
        pair = every[at : at + 2]
        block = jnp.concatenate([scenario(mate(step)) for step in pair], axis=1)
        both = dot_pieces(x_parts, pieces(block, 3), NN)
        for i, step in enumerate(pair):
            src[step] = both[:, i * scen : (i + 1) * scen]
        if not waited:
            pl.semaphore_wait(barrier, len(order))
            waited = True
        for step in pair:
            if step:
                copy(step).start()
    total = src[0]
    for step in order:
        copy(step).wait_recv()
    for step in order:
        total = total + dst[step]
    out_ref[...] = total.T
    for step in order:
        copy(step).wait_send()


def heads_of(responses, picks, flows, groups):
    nodes, cols = responses.shape
    scen = picks.shape[0] // groups
    dma = pltpu.SemaphoreType.DMA
    vmem = pl.BlockSpec(memory_space=pltpu.VMEM)
    return pl.pallas_call(
        functools.partial(heads_kernel, groups),
        name="heads",
        out_shape=jax.ShapeDtypeStruct((scen, nodes), F32),
        in_specs=[vmem] * 3,
        out_specs=vmem,
        scratch_shapes=[
            pltpu.VMEM((groups, nodes, scen), F32),
            pltpu.VMEM((groups, nodes, scen), F32),
            dma((groups,)),
            dma((groups,)),
        ],
        compiler_params=pltpu.CompilerParams(
            collective_id=1, has_side_effects=True, vmem_limit_bytes=48 << 20
        ),
    )(responses, picks.T, flows.T)


def per_device(
    diagonal, edge_ends, edge_cond, bnd_nodes, bnd_cond, hyd_ids, warm_start, scen_picks, scen_flows
):
    residual, image, packed, diagonals = moments(
        diagonal,
        edge_ends,
        edge_cond,
        bnd_nodes,
        bnd_cond,
        hyd_ids,
        warm_start,
        lax.axis_size("net"),
    )
    responses = update(warm_start, residual, image, packed, diagonals)
    heads = heads_of(responses, scen_picks, scen_flows, lax.axis_size("hyd"))
    return responses, heads


def solution(mesh):
    placed = (
        P("net"),
        P("net", None),
        P("net"),
        P("net", None, None),
        P("net", None, None),
        P("hyd"),
        P("net", "hyd"),
        P(),
        P(),
    )
    return jax.shard_map(
        per_device,
        mesh=mesh,
        in_specs=placed,
        out_specs=(P("net", "hyd"), P("hyd", "net")),
        check_vma=False,
    )
```

time: 1600 us -> 136 us (0.09)
  waiting for transfers between devices: 1310 us -> 0 us
  other arithmetic: 176 us -> 0 us
  Pallas kernels: 0 us -> 130 us
  matrix products: 36.6 us -> 0 us
  starting transfers between devices: 21.6 us -> 0 us
  local copies, waits for them, and re-layouts: 25.2 us -> 4.18 us
  between operations: 18.8 us -> 0.71 us
    psum x3 -> x0, waiting for transfers between devices: 1220 us -> none  [the longest x2 819 us: residual_sum(): return lax.psum(gram_of(residual, residual), 'net')]
    another operation x28 -> x0, other arithmetic: 165 us -> none  [the longest x21 105 us: solve_spd(): factor = jnp.linalg.cholesky(matrix)]
    pallas_call x0 -> x3, Pallas kernels: none -> 130 us  [the longest x1 61.1 us: moments(): pl.pallas_call(functools.partial(moments_kernel, nz), name='moments', out...]
    all_gather x1 -> x0, waiting for transfers between devices: 83.2 us -> none  [per_device(): lax.all_gather(iterate, 'hyd', axis=1, tiled=True)]
    dot_general x13 -> x0, matrix products: 24.7 us -> none  [the longest x1 7.65 us: per_device(): lax.dot_general(scenario, lax.all_gather(iterate, 'hyd', axis=1, tiled=Tr...]
    ppermute x6 -> x0, starting transfers between devices: 21.2 us -> none  [the longest x3 11.4 us: padded(): before = lax.ppermute(last, axis, up)]
  transfers between devices with their start and end apart: 10 -> 0, of which waited for: 5 -> 0; matrix products, arithmetic and copies ran while one was open for 3% -> 0% of each run, Pallas kernels for 0% -> 0%
where the time goes in v1:
time: 136 us; the launch traced here: 135 us
  Pallas kernels  130 us (96%)
  local copies, waits for them, and re-layouts  4.18 us (3%)
    pallas_call x1, Pallas kernels, moments(): pl.pallas_call(functools.partial(moments_kernel, nz), name='moments', out...  61.1 us
    pallas_call x1, Pallas kernels, update(): pl.pallas_call(update_kernel, name='update', out_shape=jax.ShapeDtypeStru...  36.7 us
    pallas_call x1, Pallas kernels, heads_of(): pl.pallas_call(functools.partial(heads_kernel, groups), name='heads', out...  32.4 us
    unnamed x23, local copies, waits for them, and re-layouts  4.18 us

profile of v1, /device:TPU:1, one launch (start us, length us, event | category | flops | bytes accessed | tf_op | source)
XLA Modules:
  0.0 135.1 jit_solution(3924734195628912970)
XLA Ops:
  0.6 0.0 copy-start.10
  0.6 0.0 copy-start.5
  0.7 0.7 copy-done.10
  1.3 0.0 copy-start.6
  1.3 0.0 copy-start.7
  1.3 0.0 copy-start.8
  1.3 0.0 copy-start.9
  1.3 0.0 copy-done.5
  1.4 0.6 copy-done.6
  2.0 0.0 copy-done.7
  2.0 0.0 copy-done.8
  2.0 0.0 copy-done.9
  2.0 0.0 copy-start
  2.0 1.0 copy-done
  3.1 0.0 copy-start.1
  3.1 61.1 %moments.1 = (f32[512,256]{1,0:T(8,128)S(1)}, f32[512,256]{1,0:T(8,128)S(1)}, f32[2,256,256]{2,1,0:T(8,128)S(1)}, f32[2,8,256]{2,1,0:T(8,128)S(1)}) custom-call(f32[1,512]{1,0:T(1,128)S(1)} %bitcast.10, s32[2,640]{1,0:T(2,128)S(1)} %bitcast.9, f32[1,640]{1,0:T(1,128)S(1)} %broadcast_in_dim.10.cond_ref, s32[2,64]{1,0:T(2,128)S(1)} %bitcast.11, ...), custom_call_target="tpu_custom_call" | custom-call | tf_op jit(solution)/shard_map/moments/pallas_call | solution.py:419
  64.2 0.0 copy-done.1
  64.2 0.0 copy-start.3
  64.3 0.0 copy-start.4
  64.3 36.7 %update.1.x_ref = f32[512,256]{1,0:T(8,128)} custom-call(f32[512,256]{1,0:T(8,128)S(1)} %copy-done.1, f32[512,256]{1,0:T(8,128)S(1)} %get-tuple-element.6.r_ref, f32[512,256]{1,0:T(8,128)S(1)} %get-tuple-element.7.q_ref, f32[2,256,256]{2,1,0:T(8,128)S(1)} %get-tuple-element.8.t_ref, f32[2,8,256]{2,1,0:T(8,128)S(1)} %get-tuple-element.9.d_ref), custom_call_target="tpu_custom_call" | custom-call | tf_op jit(solution)/shard_map/update/pallas_call | solution.py:535
  101.0 0.0 copy-done.3
  101.0 0.0 copy-done.4
  101.0 0.0 copy-start.2
  101.0 1.0 copy-done.2
  102.0 32.4 %heads.1 = f32[128,512]{1,0:T(8,128)S(1)} custom-call(f32[512,256]{1,0:T(8,128)S(1)} %copy-done.2, s32[4,1024]{1,0:T(4,128)S(1)} %bitcast.7, f32[4,1024]{1,0:T(4,128)S(1)} %bitcast.8), custom_call_target="tpu_custom_call" | custom-call | tf_op jit(solution)/shard_map/heads/pallas_call | solution.py:612
  134.4 0.7 copy.12
  (1 shorter events, 0.0 us)
Async XLA Ops:
  0.6 0.7 copy-start.10
  0.6 0.7 copy-start.5
  1.3 0.7 copy-start.6
  1.3 0.7 copy-start.7
  1.3 0.7 copy-start.8
  1.3 0.7 copy-start.9
  2.0 1.0 copy-start
  3.1 61.1 %copy-start.1 = (f32[512,256]{1,0:T(8,128)S(1)}, f32[512,256]{1,0:T(8,128)}, u32[]{:S(2)}) copy-start(f32[512,256]{1,0:T(8,128)} %x_ref.3) | copy-start | bytes 1572868
  64.2 36.7 %copy-start.3 = (s32[1024,4]{0,1:T(4,128)S(1)}, s32[1024,4]{0,1:T(4,128)}, u32[]{:S(2)}) copy-start(s32[1024,4]{0,1:T(4,128)} %param.16) | copy-start | bytes 49156
  64.3 36.7 %copy-start.4 = (f32[1024,4]{0,1:T(4,128)S(1)}, f32[1024,4]{0,1:T(4,128)}, u32[]{:S(2)}) copy-start(f32[1024,4]{0,1:T(4,128)} %param.17) | copy-start | bytes 49156
  101.0 1.0 copy-start.2
